TPU v7x, 32 devices: a whole 2x2x4 slice. The times are simulated.
32 devices in a mesh: groups: 2 (over x), tm: 16 (over z, y, core).
Axes of the slice: x: 2, y: 2, z: 4, core: 2. Of those that a mesh axis runs over, the one named last changes fastest.
Arguments:
- tokens: bfloat16 [8192, 1024], P(('groups', 'tm')), parts along dimension 0, may hold values from -16 to 16
- log_decay: float32 [8, 8192], P(None, ('groups', 'tm')), parts along dimension 1, may hold values from -1.5 to 0
- mem_index: int32 [64, 8], P(('groups', 'tm')), parts along dimension 0, may hold values from 0 to 29, as said below
- mem_count: int32 [64], P(('groups', 'tm')), parts along dimension 0, may hold values from 0 to 8
- w_rq: bfloat16 [1024, 512], replicated, may hold values from -0.1875 to 0.1875
- w_rk: bfloat16 [1024, 512], replicated, may hold values from -0.1875 to 0.1875
- w_rv: bfloat16 [1024, 1024], replicated, may hold values from -0.1875 to 0.1875
- norm_gain: float32 [1024], replicated, may hold values from 0.5 to 1.5
- w_mq: bfloat16 [1024, 512], replicated, may hold values from -1 to 1
- w_mk: bfloat16 [1024, 512], replicated, may hold values from -1 to 1
- w_mv: bfloat16 [1024, 512], replicated, may hold values from -0.1875 to 0.1875
- w_out: bfloat16 [512, 1024], replicated, may hold values from -0.25 to 0.25
Outputs:
- layer_out: bfloat16 [8192, 1024], P(('groups', 'tm')), parts along dimension 0
There are 2 independent parts, one for each index of `groups`. A program takes and returns all parts, laid end to end along the dimension named above; an argument that names none is the same for every part. Nothing has to cross between parts.
Inputs may be any that keep to these rules, and one draw needn't show every extreme that they name: `mem_index`: entries i < mem_count[f] of frame f's list are distinct frames held by lower indices of tm than frame f's own; all the live entries of the 2 frames of one index of tm name at most one frame of any other index.
All inputs are finite; a program needn't handle non-finite values.
Results may differ from a plain program's by a relative error of at most 0.04.
Values may be sent and summed in bfloat16 or wider, within the bound.
A program may use at most 128 MiB of HBM per device.

v0:
```python
import jax
import jax.numpy as jnp
from jax import lax
from jax.sharding import PartitionSpec as P

H = 8
DK = 64
DV = 128
MH = 4
MD = 128
MC = 512
P_SIZE = 128
BLK = 64
MEM = 8


HIGHEST = lax.Precision.HIGHEST


def entering(x, axis, combine, identity):
    length, position = (lax.axis_size(axis), lax.axis_index(axis))
    everything = jax.tree.map(lambda part: lax.all_gather(part, axis), x)
    start = jax.tree.map(
        lambda part, zero: jnp.broadcast_to(jnp.asarray(zero, part.dtype), part.shape), x, identity
    )

    def hop(k, before):
        reached = k < position
        new = combine(before, jax.tree.map(lambda part: part[k], everything))
        return jax.tree.map(lambda a, b: jnp.where(reached, a, b), new, before)

    return lax.fori_loop(0, length, hop, start)


def dilation_stride(queries, keys_rec, values_rec, decays, state):
    cumulated = jnp.cumsum(decays, axis=-1)
    length = decays.shape[-1]
    lower = jnp.arange(length)[:, None] >= jnp.arange(length)[None, :]
    gaps = cumulated[..., :, None] - cumulated[..., None, :]
    weight_tensors = jnp.where(lower, jnp.exp(jnp.where(lower, gaps, 0.0)), 0.0)
    scores = jnp.einsum("bhtd,bhsd->bhts", queries, keys_rec, precision=HIGHEST) * weight_tensors
    inner = jnp.einsum("bhts,bhsv->bhtv", scores, values_rec, precision=HIGHEST)
    carried = jnp.exp(cumulated)[..., None] * jnp.einsum(
        "bhtd,bhdv->bhtv", queries, state, precision=HIGHEST
    )
    tail_decay = jnp.exp(cumulated[..., -1:] - cumulated)
    new_state = jnp.exp(cumulated[..., -1])[..., None, None] * state + jnp.einsum(
        "bhsd,bhsv->bhdv", keys_rec * tail_decay[..., None], values_rec, precision=HIGHEST
    )
    return (inner + carried, new_state, cumulated)


def state_step(keys_rec, values_rec, decays, state):
    cumulated = jnp.cumsum(decays, axis=-1)
    tail_decay = jnp.exp(cumulated[..., -1:] - cumulated)
    new_state = jnp.exp(cumulated[..., -1])[..., None, None] * state + jnp.einsum(
        "bhsd,bhsv->bhdv", keys_rec * tail_decay[..., None], values_rec, precision=HIGHEST
    )
    return (new_state, cumulated[..., -1])


def combine_states(earlier, later):
    return (earlier[0] + later[0], jnp.exp(later[0])[..., None, None] * earlier[1] + later[1])


def carry_across(total_decay, local_state):
    identity = (jnp.zeros_like(total_decay), jnp.zeros_like(local_state))
    return entering((total_decay, local_state), "tm", combine_states, identity)


def on_device(
    tokens, log_decay, mem_index, mem_count, w_rq, w_rk, w_rv, norm_gain, w_mq, w_mk, w_mv, w_out
):
    row_count = tokens.shape[0]
    frame_count = row_count // P_SIZE

    def project(weight):
        return jnp.dot(tokens, weight, preferred_element_type=jnp.float32).astype(jnp.bfloat16)

    def heads(values, width):
        return (
            values.astype(jnp.float32)
            .reshape(frame_count, 2, BLK, H, width)
            .transpose(0, 1, 3, 2, 4)
        )

    queries = heads(project(w_rq), DK) * DK ** (-0.5)
    keys_rec = heads(project(w_rk), DK)
    values_rec = heads(project(w_rv), DV)
    decays = log_decay.reshape(H, frame_count, 2, BLK).transpose(1, 2, 0, 3)
    zero_state = jnp.zeros((2, H, DK, DV), jnp.float32)
    zero_total = jnp.zeros((2, H), jnp.float32)

    def summarize(carry, inputs):
        state, overall_total_aggregate = carry
        frame_k, frame_v, frame_d = inputs
        new_state, frame_number = state_step(frame_k, frame_v, frame_d, state)
        return ((new_state, overall_total_aggregate + frame_number), None)

    (local_state, local_total), unused_out = lax.scan(
        summarize, (zero_state, zero_total), (keys_rec, values_rec, decays)
    )
    incoming_total, incoming_state = carry_across(local_total, local_state)

    def advance(state, inputs):
        frame_q, frame_k, frame_v, frame_d = inputs
        output, new_state, cumulated = dilation_stride(frame_q, frame_k, frame_v, frame_d, state)
        return (new_state, output)

    last_state, outputs = lax.scan(advance, incoming_state, (queries, keys_rec, values_rec, decays))
    scale = lax.rsqrt(jnp.mean(outputs * outputs, axis=-1, keepdims=True) + 1e-05)
    normed = (outputs * scale).transpose(0, 1, 3, 2, 4).reshape(row_count, H * DV) * norm_gain
    hidden = (tokens.astype(jnp.float32) + normed).astype(jnp.bfloat16)

    def mem_project(weight):
        return (
            jnp.dot(hidden, weight, preferred_element_type=jnp.float32)
            .astype(jnp.bfloat16)
            .reshape(frame_count, P_SIZE, MC)
        )

    mem_q = mem_project(w_mq)
    mem_k = mem_project(w_mk)
    mem_v = mem_project(w_mv)
    owners = lax.axis_size("tm")
    slot_live = jnp.arange(MEM, dtype=jnp.int32)[None, :] < mem_count[:, None]
    owner_of = mem_index // frame_count
    local_of = mem_index % frame_count
    owner_ids = jnp.arange(owners, dtype=jnp.int32)
    hits = (owner_of.reshape(-1)[:, None] == owner_ids[None, :]) & slot_live.reshape(-1)[:, None]
    wanted_here = jnp.max(jnp.where(hits, local_of.reshape(-1)[:, None], 0), axis=0)
    wanted = lax.all_to_all(wanted_here[:, None], "tm", split_axis=0, concat_axis=0, tiled=True)[
        :, 0
    ]
    outgoing_keys_table = jnp.take(mem_k, wanted, axis=0)
    send_values = jnp.take(mem_v, wanted, axis=0)
    query_rows = mem_q.reshape(frame_count, P_SIZE, MH, MD)
    slot_of = jnp.arange((MEM + 1) * P_SIZE, dtype=jnp.int32) // P_SIZE
    key_live = (slot_of[None, :] == 0) | (slot_of[None, :] - 1 < mem_count[:, None])
    got_keys, got_values = (
        lax.all_to_all(outgoing_keys_table, "tm", split_axis=0, concat_axis=0, tiled=True),
        lax.all_to_all(send_values, "tm", split_axis=0, concat_axis=0, tiled=True),
    )
    keys_all = jnp.concatenate([mem_k[:, None], jnp.take(got_keys, owner_of, axis=0)], axis=1)
    keys_all = keys_all.reshape(frame_count, (MEM + 1) * P_SIZE, MH, MD)
    scores = jnp.einsum(
        "fqhd,fkhd->fhqk", query_rows, keys_all, preferred_element_type=jnp.float32
    ) * MD ** (-0.5)
    scores = jnp.where(key_live[:, None, None, :], scores, -1e30)
    peak = jnp.max(scores, axis=-1, keepdims=True)
    expo = jnp.exp(scores - peak)
    probs = (expo / jnp.sum(expo, axis=-1, keepdims=True)).astype(jnp.bfloat16)
    values_all = jnp.concatenate([mem_v[:, None], jnp.take(got_values, owner_of, axis=0)], axis=1)
    values_all = values_all.reshape(frame_count, (MEM + 1) * P_SIZE, MH, MD)
    mixed = jnp.einsum("fhqk,fkhd->fqhd", probs, values_all, preferred_element_type=jnp.float32)
    attended = mixed.reshape(row_count, MC).astype(jnp.bfloat16)
    projected = jnp.dot(attended, w_out, preferred_element_type=jnp.float32)
    return (hidden.astype(jnp.float32) + projected).astype(jnp.bfloat16)


def solution(mesh):
    placed = (
        P(("groups", "tm"), None),
        P(None, ("groups", "tm")),
        P(("groups", "tm"), None),
        P(("groups", "tm")),
        P(),
        P(),
        P(),
        P(),
        P(),
        P(),
        P(),
        P(),
    )
    return jax.shard_map(
        on_device, mesh=mesh, in_specs=placed, out_specs=P(("groups", "tm"), None), check_vma=False
    )
```

profile of v0, /device:TPU:25, one launch (start us, length us, event | category | flops | bytes accessed | tf_op | source)
XLA Modules:
  0.0 288.3 jit_solution(13836829489433879310)
XLA Ops:
  6.5 1.6 copy-done
  8.1 1.7 fusion.32
  11.3 1.2 fusion.35
  12.5 1.2 reshape.164
  13.8 1.3 copy.64
  15.2 5.0 %while.40 = (s32[]{:T(128)}, f32[2,8,64,128]{3,2,1,0:T(8,128)S(1)}, f32[2,8]{1,0:T(2,128)S(1)}, f32[2,2,8,64]{3,2,1,0:T(8,128)S(1)}, f32[2,2,8,64,64]{3,4,2,1,0:...) while((s32[]{:T(128)}, f32[2,8,64,128]{3,2,1,0:T(8,128)S(1)}, ...), condition=%wide.region_2.3_spmd.clone, body=%wide.region_0.2_spmd.clone.sunk | while | flops 101187616 | bytes 2132528 | solution.py:100
  16.0 1.8 convolution_add_fusion.6
  18.5 1.8 convolution_add_fusion.6
  20.3 0.8 copy-done.3
  21.6 0.7 copy.71
  22.2 6.4 %all-to-all-start = ((s32[16,1,1]{2,1,0:T(1,128)}), s32[16,1,1]{2,1,0:T(1,128)S(1)}, u32[]{:S(2)}, u32[]{:S(2)}) async-start(s32[16,1,1]{2,1,0:T(1,128)} %copy.71), calls=%async_computation | async-start | bytes 16384 | tf_op jit(solution)/shard_map/all_to_all | solution.py:132
  28.6 17.0 %all-gather.2 = f32[16,2,8]{2,1,0:T(2,128)S(1)} all-gather(f32[1,2,8]{2,1,0:T(2,128)S(1)} %bitcast.144), channel_id=2, replica_groups=mesh['groups'=2,'tm'=16] {'tm'}, dimensions={0}, use_global_device_ids=true | all-gather | bytes 1088 | tf_op jit(solution)/shard_map/all_gather | solution.py:22
  45.7 1.7 fusion.34
  47.3 1.2 mul.104
  48.5 1.4 copy.114
  50.4 45.5 %all-gather.5.cloned.1.call-done = f32[32,8,64,128]{3,2,1,0:T(8,128)} async-done(((f32[2,8,64,128]{3,2,1,0:T(8,128)}), f32[32,8,64,128]{3,2,1,0:T(8,128)}) %all-gather.5.cloned.1.call-update) | async-done | bytes 8388624 | tf_op jit(solution)/shard_map/all_gather | solution.py:22
  95.8 19.4 %while.41 = (s32[]{:T(128)}, f32[2,8,64,128]{3,2,1,0:T(8,128)S(1)}, s32[]{:T(128)}, f32[16,2,8]{2,1,0:T(2,128)S(1)}, f32[16,2,8,64,128]{4,3,2,1,0:T(8,128)}, /*index=5*/s32[]{:T(128)}, s32[]{:T(128)}) while((s32[]{:T(128)}, f32[2,8,64,128]{3,2,1,0:T(8,128)S(1)}, s32[]{:T(128)}, f32[16,2,8]{2,1,0:T(2,128)S(1)}, ...), condition=%wide.region_4.5_spmd.clone, body=%wide.region_3.4_spmd.clone.sunk | while | flops 524292 | bytes 1573161 | solution.py:32
  95.8 1.2 fusion.104
  97.1 1.2 fusion.104
  98.3 1.2 fusion.104
  99.5 1.2 fusion.104
  100.7 1.2 fusion.104
  101.9 1.2 fusion.104
  103.1 1.2 fusion.104
  104.3 1.2 fusion.104
  105.6 1.2 fusion.104
  106.8 1.2 fusion.104
  108.0 1.2 fusion.104
  109.2 1.2 fusion.104
  110.4 1.2 fusion.104
  111.6 1.2 fusion.104
  112.8 1.2 fusion.104
  114.1 1.2 fusion.104
  115.2 13.1 %while.39 = (s32[]{:T(128)}, f32[2,8,64,128]{3,2,1,0:T(8,128)S(1)}, f32[2,2,8,64,128]{4,3,2,1,0:T(8,128)}, f32[2,2,8,64]{3,2,1,0:T(8,128)S(1)}, f32[2,2,8,64,64]...) while((s32[]{:T(128)}, f32[2,8,64,128]{3,2,1,0:T(8,128)S(1)}, ...), condition=%wide.region_7.8_spmd, body=%wide.region_5.7_spmd.sunk | while | flops 353243136 | bytes 16067053 | solution.py:110
  115.7 1.2 constant_dynamic-slice_fusion.2
  116.9 1.0 convolution_multiply_fusion.4
  117.9 0.6 fusion.101
  118.8 0.7 fusion.102
  119.5 1.0 copy-done.7
  120.5 1.3 convolution_add_fusion.5
  122.3 1.2 constant_dynamic-slice_fusion.2
  123.5 1.0 convolution_multiply_fusion.4
  124.5 0.6 fusion.101
  125.4 0.7 fusion.102
  126.1 1.0 copy-done.7
  127.0 1.3 convolution_add_fusion.5
  128.3 1.6 multiply_reduce_fusion
  129.9 1.6 multiply_bitcast_fusion
  133.9 2.0 gather_fusion
  135.9 2.0 gather_fusion.2
  138.0 4.0 %broadcast_select_fusion.1 = (bf16[16,128,512]{2,1,0:T(8,128)(2,1)}, bf16[16,128,512]{2,1,0:T(8,128)(2,1)S(1)}) fusion(bf16[16,128,512]{2,1,0:T(8,128)(2,1)} %gather_fusion, pred[16]{0:T(512)(128)(4,1)S(1)} %compare_and_fusion.1, bf16[16,128,512]{2,1,0:T(8,128)(2,1)} %gather_fusion.2), kind=kLoop, calls=%fused_computation.58 | loop fusion | flops 2097152 | bytes 8388624 | tf_op jit(solution)/shard_map/jit(_take)/select_n | solution.py:136
  142.0 51.5 %all_to_all.19 = bf16[16,128,512]{2,1,0:T(8,128)(2,1)} all-to-all(bf16[16,128,512]{2,1,0:T(8,128)(2,1)S(1)} %get-tuple-element.311), channel_id=1, replica_groups=mesh['groups'=2,'tm'=16] {'tm'}, dimensions={0} | all-to-all | bytes 4194304 | tf_op jit(solution)/shard_map/all_to_all | solution.py:141
  193.5 6.2 %all-to-all-start.1 = ((bf16[16,128,512]{2,1,0:T(8,128)(2,1)}), bf16[16,128,512]{2,1,0:T(8,128)(2,1)}, u32[]{:S(2)}, u32[]{:S(2)}) async-start(bf16[16,128,512]{2,1,0:T(8,128)(2,1)} %get-tuple-element.310), calls=%async_computation.1 | async-start | bytes 4194304 | tf_op jit(solution)/shard_map/all_to_all | solution.py:142
  200.4 3.6 %gather_fusion.3 = bf16[16,128,512]{2,1,0:T(8,128)(2,1)} fusion(bf16[16,128,512]{2,1,0:T(8,128)(2,1)} %all_to_all.19, s32[1024]{0:T(1024)S(1)} %pad_clamp_fusion), kind=kCustom, calls=%fused_computation.3.clone | custom fusion | bytes 4194368 | tf_op jit(solution)/shard_map/jit(_take)/gather | solution.py:144
  204.0 39.9 %all-to-all-done.1 = bf16[16,128,512]{2,1,0:T(8,128)(2,1)} async-done(((bf16[16,128,512]{2,1,0:T(8,128)(2,1)}), bf16[16,128,512]{2,1,0:T(8,128)(2,1)}, u32[]{:S(2)}, u32[]{:S(2)}) %all-to-all-start.1) | async-done | bytes 2097184 | tf_op jit(solution)/shard_map/all_to_all | solution.py:142
  243.9 3.6 %gather_fusion.1 = bf16[16,128,512]{2,1,0:T(8,128)(2,1)} fusion(bf16[16,128,512]{2,1,0:T(8,128)(2,1)} %all-to-all-done.1, s32[1024]{0:T(1024)S(1)} %pad_clamp_fusion), kind=kCustom, calls=%fused_computation.1.clone | custom fusion | bytes 4194368 | tf_op jit(solution)/shard_map/jit(_take)/gather | solution.py:153
  247.5 2.7 broadcast_select_fusion.3
  250.2 2.4 pad_maximum_fusion
  252.5 5.3 %reshape.163 = bf16[2,1152,4,128]{3,2,1,0:T(4,128)(2,1)} reshape(bf16[2,9,128,512]{3,2,1,0:T(8,128)(2,1)} %get-tuple-element.313) | data formatting | bytes 4718592 | tf_op jit(solution)/shard_map/reshape | solution.py:145
  257.8 4.8 %fusion.26 = f32[2,4,128,1152]{3,2,1,0:T(8,128)} fusion(bf16[2,1152,4,128]{3,2,1,0:T(4,128)(2,1)} %reshape.163, pred[2,1152]{1,0:T(4,128)(4,1)S(1)} %compare_or_fusion, bf16[2,128,4,128]{3,2,1,0:T(4,128)(2,1)S(1)} %reshape_reshape.3), kind=kOutput, calls=%fused_computation.49 | convolution fusion | flops 304349184 | bytes 7342336 | tf_op jit(solution)/shard_map/fqhd,fkhd->fhqk/dot_general | solution.py:146
  262.6 3.5 %exponential_reduce_fusion = f32[2,4,128]{2,1,0:T(4,128)S(1)} fusion(bf16[2,1152,4,128]{3,2,1,0:T(4,128)(2,1)} %reshape.163, pred[2,1152]{1,0:T(4,128)(4,1)S(1)} %compare_or_fusion, bf16[2,128,4,128]{3,2,1,0:T(4,128)(2,1)S(1)} %reshape_reshape.3), kind=kOutput, calls=%fused_computation.51 | convolution fusion | flops 306709632 | bytes 2627840 | tf_op jit(solution)/shard_map/sub | solution.py:151
  266.1 5.3 %reshape.161 = bf16[2,1152,4,128]{3,2,1,0:T(4,128)(2,1)} reshape(bf16[2,9,128,512]{3,2,1,0:T(8,128)(2,1)} %get-tuple-element.312) | data formatting | bytes 4718592 | tf_op jit(solution)/shard_map/reshape | solution.py:154
  271.5 7.3 %fusion.39 = bf16[2,128,4,128]{1,3,2,0:T(8,128)(2,1)S(1)} fusion(f32[2,4,128]{2,1,0:T(4,128)S(1)} %exponential_reduce_fusion, bf16[2,1152,4,128]{3,2,1,0:T(4,128)(2,1)} %reshape.161, f32[2,4,128,1152]{3,2,1,0:T(8,128)} %fusion.26), kind=kOutput, calls=%fused_computation.75 | convolution fusion | flops 305662080 | bytes 7344128 | tf_op jit(solution)/shard_map/fhqk,fkhd->fqhd/dot_general | solution.py:155
  279.0 2.5 fusion.30
  (106 shorter events, 8.6 us)
Async XLA Ops:
  6.5 1.6 copy-start
  6.5 89.3 %all-gather.5.cloned.1.call-start = ((), (), s32[]{:S(2)}) async-start(), calls=%async_computation.3 | async-start | bytes 8912896 | tf_op jit(solution)/shard_map/all_gather | solution.py:22
  9.9 1.0 copy-start.4
  9.9 1.4 copy-start.11
  11.3 3.8 %copy-start.12 = (f32[8,256]{1,0:T(8,128)S(1)}, f32[8,256]{1,0:T(8,128)}, u32[]{:S(2)}) copy-start(f32[8,256]{1,0:T(8,128)} %param.23) | copy-start | bytes 24580
  13.8 1.5 copy-start.2
  15.2 5.9 %copy-start.14 = (s32[2,8]{1,0:T(2,128)S(1)}, s32[2,8]{1,0:T(2,128)}, u32[]{:S(2)}) copy-start(s32[2,8]{1,0:T(2,128)} %param.24) | copy-start | bytes 196
  15.2 6.1 %copy-start.15 = (s32[2]{0:T(128)S(1)}, s32[2]{0:T(128)}, u32[]{:S(2)}) copy-start(s32[2]{0:T(128)} %param.25) | copy-start | bytes 28
  20.3 0.8 copy-start.3
  22.2 27.7 %all-to-all-start = ((s32[16,1,1]{2,1,0:T(1,128)}), s32[16,1,1]{2,1,0:T(1,128)S(1)}, u32[]{:S(2)}, u32[]{:S(2)}) async-start(s32[16,1,1]{2,1,0:T(1,128)} %copy.71), calls=%async_computation | async-start | bytes 16384 | tf_op jit(solution)/shard_map/all_to_all | solution.py:132
  115.7 3.1 %copy-start.6 = (f32[2,2,8,64,128]{4,3,2,1,0:T(8,128)S(1)}, f32[2,2,8,64,128]{4,3,2,1,0:T(8,128)}, u32[]{:S(2)}) copy-start(f32[2,2,8,64,128]{4,3,2,1,0:T(8,128)} %get-tuple-element.492) | copy-start | bytes 3145732 | tf_op jit(solution)/shard_map/while
  119.5 1.0 copy-start.7
  122.3 3.1 %copy-start.6 = (f32[2,2,8,64,128]{4,3,2,1,0:T(8,128)S(1)}, f32[2,2,8,64,128]{4,3,2,1,0:T(8,128)}, u32[]{:S(2)}) copy-start(f32[2,2,8,64,128]{4,3,2,1,0:T(8,128)} %get-tuple-element.492) | copy-start | bytes 3145732 | tf_op jit(solution)/shard_map/while
  126.0 1.0 copy-start.7
  129.9 2.3 copy-start.5
  129.9 2.3 copy-start.13
  131.5 1.2 copy-start.8
  132.2 1.3 copy-start.9
  193.5 6.4 %copy-start.10 = (bf16[1024,512]{1,0:T(8,128)(2,1)S(1)}, bf16[1024,512]{1,0:T(8,128)(2,1)}, u32[]{:S(2)}) copy-start(bf16[1024,512]{1,0:T(8,128)(2,1)} %param.30) | copy-start | bytes 3145732
  193.5 50.4 %all-to-all-start.1 = ((bf16[16,128,512]{2,1,0:T(8,128)(2,1)}), bf16[16,128,512]{2,1,0:T(8,128)(2,1)}, u32[]{:S(2)}, u32[]{:S(2)}) async-start(bf16[16,128,512]{2,1,0:T(8,128)(2,1)} %get-tuple-element.310), calls=%async_computation.1 | async-start | bytes 4194304 | tf_op jit(solution)/shard_map/all_to_all | solution.py:142
  271.5 10.0 %copy-start.1 = (bf16[1024,1024]{1,0:T(8,128)(2,1)S(1)}, bf16[1024,1024]{1,0:T(8,128)(2,1)}, u32[]{:S(2)}) copy-start(bf16[1024,1024]{1,0:T(8,128)(2,1)} %param.28) | copy-start | bytes 6291460
Sparse Core Ops, SparseCore 0:
  21.2 74.5 all-gather.4
where the time goes:
time: 294 us; the launch traced here: 288 us
  waiting for transfers between devices  85.4 us (29%)
  blocking collectives  68.6 us (23%)
  local copies, waits for them, and re-layouts  38.3 us (13%)
  matrix products  34.8 us (12%)
  other arithmetic  34.2 us (12%)
  between operations  13.7 us (5%)
  starting transfers between devices  12.6 us (4%)
    all_to_all x1, blocking collectives, on_device(): lax.all_to_all(outgoing_keys_table, 'tm', split_axis=0, concat_axis=0, ti...  51.5 us
    all_gather x1, waiting for transfers between devices, entering(): everything = jax.tree.map(lambda part: lax.all_gather(part, axis), x)  45.5 us
    all_to_all x1, waiting for transfers between devices, on_device(): lax.all_to_all(send_values, 'tm', split_axis=0, concat_axis=0, tiled=True)  39.9 us
    select_n x16, other arithmetic, hop(): return jax.tree.map(lambda a, b: jnp.where(reached, a, b), new, before)  18.8 us
    all_gather x1, blocking collectives, entering(): everything = jax.tree.map(lambda part: lax.all_gather(part, axis), x)  17 us
    dot_general x1, matrix products, on_device(): jnp.einsum('fhqk,fkhd->fqhd', probs, values_all, preferred_element_type=j...  7.29 us
    all_to_all x1, starting transfers between devices, on_device(): lax.all_to_all(wanted_here[:, None], 'tm', split_axis=0, concat_axis=0, t...  6.39 us
    all_to_all x1, starting transfers between devices, on_device(): lax.all_to_all(send_values, 'tm', split_axis=0, concat_axis=0, tiled=True)  6.17 us
  transfers between devices with their start and end apart: 3, of which 2 were waited for; matrix products, arithmetic and copies ran while one was open for 3% of the time, Pallas kernels for 0%

commit v1 on v0

v1 whole, which is shorter than its diff:
```python
import functools

import jax
import jax.numpy as jnp
from jax import lax
from jax.experimental import pallas as pl
from jax.experimental.pallas import tpu as pltpu
from jax.sharding import PartitionSpec as P

H = 8
DK = 64
DV = 128
MH = 4
MD = 128
MC = 512
P_SIZE = 128
BLK = 64
MEM = 8
PLANE = 4
EXTRA = 16
NEG = -1e30
HIGHEST = lax.Precision.HIGHEST
F32 = jnp.float32
BF16 = jnp.bfloat16
NT = (((1,), (1,)), ((), ()))
TN = (((0,), (0,)), ((), ()))


def dot(a, b, dims=(((1,), (0,)), ((), ())), precision=None):
    return lax.dot_general(a, b, dims, precision=precision, preferred_element_type=F32)


def kernel(
    n,
    idx_ref,
    cnt_ref,
    tok_ref,
    ld_ref,
    wrq_ref,
    wrk_ref,
    wrv_ref,
    gain_ref,
    wmq_ref,
    wmk_ref,
    wmv_ref,
    wout_ref,
    out_ref,
    msg_out,
    msg_in,
    pre_out,
    state_in,
    kv,
    k_s,
    v_s,
    q_s,
    o_s,
    hid_s,
    mq_s,
    sel_s,
    m_s,
    l_s,
    acc_s,
    send1,
    recv1,
    send2,
    recv2,
    send_kv,
    recv_kv,
):
    rows = tok_ref.shape[0]
    fpd = rows // P_SIZE
    slice_rows = pre_out.shape[1]
    planes = n // PLANE
    me = lax.axis_index("tm")
    z = me // PLANE
    p = me % PLANE
    core_mate = z * PLANE + (p + 1 - 2 * (p % 2))
    p_y = (p + 2) % PLANE
    y_mate = z * PLANE + p_y

    barrier = pltpu.get_barrier_semaphore()

    def greet(i, carry):
        pl.semaphore_signal(barrier, inc=1, device_id={"tm": (me + i) % n})
        return carry

    lax.fori_loop(1, n, greet, 0)

    tok = tok_ref[...]
    k_s[...] = dot(tok, wrk_ref[...]).astype(BF16)
    v_s[...] = dot(tok, wrv_ref[...]).astype(BF16)

    t_id = lax.broadcasted_iota(jnp.int32, (rows, rows), 0)
    s_id = lax.broadcasted_iota(jnp.int32, (rows, rows), 1)
    same = (t_id // BLK) % 2 == (s_id // BLK) % 2
    causal = same & (t_id >= s_id)
    causal_f = jnp.where(causal, 1.0, 0.0).astype(F32)
    same_f = jnp.where(same, 1.0, 0.0).astype(F32)
    ld = ld_ref[...]
    cum_col = dot(causal_f, ld, NT, HIGHEST)
    cum_row = dot(ld, causal_f, NT, HIGHEST)
    total_col = dot(same_f, ld, NT, HIGHEST)
    tail = jnp.exp(total_col - cum_col)
    reach = jnp.exp(cum_col)
    lane = lax.broadcasted_iota(jnp.int32, (rows, 2 * DK), 1)
    chain = (lax.broadcasted_iota(jnp.int32, (rows, 2 * DK), 0) // BLK) % 2
    first_head = lane < DK
    unit_row = lax.broadcasted_iota(jnp.int32, (2 * DK, DV), 0)
    extra_row = lax.broadcasted_iota(jnp.int32, (EXTRA, DV), 0)
    per_unit = DK // slice_rows
    for b in range(2):
        chain_f = jnp.where(chain == b, 1.0, 0.0).astype(F32)
        total = dot(ld, chain_f, precision=HIGHEST)
        for pair in range(H // 2):
            at = pl.ds(pair * 2 * DK, 2 * DK)
            weight = jnp.where(
                first_head, tail[:, 2 * pair : 2 * pair + 1], tail[:, 2 * pair + 1 : 2 * pair + 2]
            )
            scaled = (k_s[:, at].astype(F32) * weight * chain_f).astype(BF16)
            both = dot(scaled, v_s[:, pl.ds(pair * 2 * DV, 2 * DV)], TN)
            state = jnp.where(unit_row < DK, both[:, :DV], both[:, DV:]).astype(BF16)
            for half in range(2):
                head = 2 * pair + half
                d = jnp.broadcast_to(total[head : head + 1, :], (EXTRA, DV))
                hi = d.astype(BF16).astype(F32)
                mid = (d - hi).astype(BF16).astype(F32)
                low = d - hi - mid
                parts = jnp.where(
                    extra_row == 0,
                    hi,
                    jnp.where(extra_row == 1, mid, jnp.where(extra_row == 2, low, 0.0)),
                ).astype(BF16)
                for piece in range(per_unit):
                    j = (b * H + head) * per_unit + piece
                    start = half * DK + piece * slice_rows
                    msg_out[j, pl.ds(0, slice_rows), :] = state[start : start + slice_rows]
                    msg_out[j, pl.ds(slice_rows, EXTRA), :] = parts

    pl.semaphore_wait(barrier, n - 1)

    def copy1(dst, slot):
        return pltpu.make_async_remote_copy(
            src_ref=msg_out.at[dst],
            dst_ref=msg_in.at[slot],
            send_sem=send1.at[dst],
            recv_sem=recv1.at[slot],
            device_id={"tm": dst},
        )

    def send_slices(i, carry):
        copy1((me + i) % n, me).start()
        return carry

    lax.fori_loop(1, n, send_slices, 0)
    msg_in[me] = msg_out[me]

    q_s[...] = (dot(tok, wrq_ref[...]).astype(BF16).astype(F32) * DK**-0.5).astype(BF16)
    for head in range(H):
        pair = head // 2
        at = pl.ds(pair * 2 * DK, 2 * DK)
        mine = first_head if head % 2 == 0 else jnp.logical_not(first_head)
        qh = jnp.where(mine, q_s[:, at].astype(F32), 0.0).astype(BF16)
        gaps = cum_col[:, head : head + 1] - cum_row[head : head + 1, :]
        decay = jnp.exp(jnp.where(causal, gaps, NEG))
        scores = (dot(qh, k_s[:, at], NT) * decay).astype(BF16)
        o_s[:, pl.ds(head * DV, DV)] = dot(scores, v_s[:, pl.ds(head * DV, DV)])

    def copy2(dst, slot):
        return pltpu.make_async_remote_copy(
            src_ref=pre_out.at[dst],
            dst_ref=state_in.at[slot],
            send_sem=send2.at[dst],
            recv_sem=recv2.at[slot],
            device_id={"tm": dst},
        )

    def hop(i, before):
        @pl.when(i != me)
        def _():
            copy1(i, i).wait_recv()

        pre_out[i] = before.astype(BF16)

        @pl.when(i != me)
        def _():
            copy2(i, me).start()

        d = msg_in[i, pl.ds(slice_rows, EXTRA), :].astype(F32)
        d = d[0:1] + d[1:2] + d[2:3]
        return jnp.exp(d) * before + msg_in[i, pl.ds(0, slice_rows), :].astype(F32)

    lax.fori_loop(0, n, hop, jnp.zeros((slice_rows, DV), F32))
    state_in[me] = pre_out[me]

    def take(i, carry):
        copy2((me + i) % n, (me + n - i) % n).wait_recv()
        return carry

    lax.fori_loop(1, n, take, 0)

    half_units = n // 2
    pair_slices = 2 * per_unit
    for head in range(H):
        pair = head // 2
        at = pl.ds(pair * 2 * DK, 2 * DK)
        mine = first_head if head % 2 == 0 else jnp.logical_not(first_head)
        qh = jnp.where(mine, q_s[:, at].astype(F32) * reach[:, head : head + 1], 0.0)
        col = pl.ds(head * DV, DV)
        o = o_s[:, col]
        for b in range(2):
            incoming = state_in[pl.ds(b * half_units + pair * pair_slices, pair_slices)]
            incoming = incoming.reshape(2 * DK, DV)
            o = o + dot(jnp.where(chain == b, qh, 0.0).astype(BF16), incoming)
        scale = lax.rsqrt(jnp.mean(o * o, axis=-1, keepdims=True) + 1e-05)
        y = o * scale * gain_ref[:, col]
        hid_s[:, col] = (tok_ref[:, col].astype(F32) + y).astype(BF16)

    hid = hid_s[...]
    kv[me, :, pl.ds(0, MC)] = dot(hid, wmk_ref[...]).astype(BF16)
    kv[me, :, pl.ds(MC, MC)] = dot(hid, wmv_ref[...]).astype(BF16)

    def copy_kv(slot, role, dst):
        return pltpu.make_async_remote_copy(
            src_ref=kv.at[slot],
            dst_ref=kv.at[slot],
            send_sem=send_kv.at[role, slot],
            recv_sem=recv_kv.at[slot],
            device_id={"tm": dst},
        )

    up = (me + PLANE) % n

    def pass_on(slot):
        @pl.when(z < planes - 1)
        def _():
            copy_kv(slot, 0, up).start()

        copy_kv(slot, 2, y_mate).start()
        copy_kv(slot, 1, core_mate).start()

    pass_on(me)

    mq_s[...] = dot(hid, wmq_ref[...]).astype(BF16)
    key_scale = MD**-0.5
    own_frame = (t_id // P_SIZE) == (s_id // P_SIZE)
    for h in range(MH):
        col = pl.ds(h * MD, MD)
        s = dot(mq_s[:, col], kv[me, :, pl.ds(h * MD, MD)], NT) * key_scale
        s = jnp.where(own_frame, s, NEG)
        m = jnp.max(s, axis=-1, keepdims=True)
        e = jnp.exp(s - m)
        m_s[h] = jnp.broadcast_to(m, (rows, 128))
        l_s[h] = jnp.broadcast_to(jnp.sum(e, axis=-1, keepdims=True), (rows, 128))
        acc_s[:, col] = dot(e.astype(BF16), kv[me, :, pl.ds(MC + h * MD, MD)])

    keys = PLANE * P_SIZE
    key_owner = lax.broadcasted_iota(jnp.int32, (P_SIZE, keys), 1) // P_SIZE

    def attend(base):
        live = []
        wants = [jnp.int32(0)] * PLANE
        for f in range(fpd):
            hit = jnp.full((P_SIZE, keys), NEG, F32)
            count = cnt_ref[f]
            for i in range(MEM):
                frame = idx_ref[f, i]
                owner = jnp.where(i < count, lax.div(frame, jnp.int32(fpd)), -1) - base
                local = lax.rem(frame, jnp.int32(fpd))
                hit = jnp.where(key_owner == owner, 0.0, hit)
                wants = [
                    jnp.where(owner == w, local, wants[w]) for w in range(PLANE)
                ]
            live.append(hit)
        bias = jnp.concatenate(live, axis=0)
        for w in range(PLANE):
            chosen = kv[base + w, pl.ds(0, P_SIZE), :]
            want = jnp.full((P_SIZE, 2 * MC), wants[w], jnp.int32)
            for f in range(1, fpd):
                chosen = jnp.where(want == f, kv[base + w, pl.ds(f * P_SIZE, P_SIZE), :], chosen)
            sel_s[pl.ds(w * P_SIZE, P_SIZE), :] = chosen
        for h in range(MH):
            col = pl.ds(h * MD, MD)
            s = dot(mq_s[:, col], sel_s[:, pl.ds(h * MD, MD)], NT) * key_scale + bias
            m_old = m_s[h][:, 0:1]
            m = jnp.maximum(m_old, jnp.max(s, axis=-1, keepdims=True))
            fade = jnp.exp(m_old - m)
            e = jnp.exp(s - m)
            m_s[h] = jnp.broadcast_to(m, (rows, 128))
            l_new = l_s[h][:, 0:1] * fade + jnp.sum(e, axis=-1, keepdims=True)
            l_s[h] = jnp.broadcast_to(l_new, (rows, 128))
            acc_s[:, col] = acc_s[:, col] * fade + dot(
                e.astype(BF16), sel_s[:, pl.ds(MC + h * MD, MD)]
            )

    def plane_step(j, carry):
        base = (z - j) * PLANE
        from_y = base + p_y
        copy_kv(from_y, 2, y_mate).wait_recv()
        copy_kv(from_y, 1, core_mate).start()

        @pl.when(j < z)
        def _():
            below = base - PLANE + p
            copy_kv(below, 0, up).wait_recv()
            pass_on(below)

        near = base + (p + 1 - 2 * (p % 2))
        copy_kv(near, 1, core_mate).wait_recv()
        diagonal = base + (p_y + 1 - 2 * (p_y % 2))
        copy_kv(diagonal, 1, core_mate).wait_recv()
        attend(base)
        return carry

    lax.fori_loop(0, z + 1, plane_step, 0)

    for h in range(MH):
        col = pl.ds(h * MD, MD)
        mq_s[:, col] = (acc_s[:, col] / l_s[h][:, 0:1]).astype(BF16)
    projected = dot(mq_s[...], wout_ref[...])
    out_ref[...] = (hid_s[...].astype(F32) + projected).astype(BF16)

    def drain(i, carry):
        dst = (me + i) % n
        copy1(dst, me).wait_send()
        copy2(dst, me).wait_send()
        return carry

    lax.fori_loop(1, n, drain, 0)

    def drain_kv(j, carry):
        base = (z - j) * PLANE

        @pl.when(z < planes - 1)
        def _():
            copy_kv(base + p, 0, up).wait_send()

        copy_kv(base + p, 2, y_mate).wait_send()
        copy_kv(base + p, 1, core_mate).wait_send()
        copy_kv(base + p_y, 1, core_mate).wait_send()
        return carry

    lax.fori_loop(0, z + 1, drain_kv, 0)


def on_device(
    n, tokens, log_decay, mem_index, mem_count, w_rq, w_rk, w_rv, norm_gain, w_mq, w_mk, w_mv, w_out
):
    rows, width = tokens.shape
    slice_rows = 2 * H * DK // n
    vmem = pl.BlockSpec(memory_space=pltpu.VMEM)
    smem = pl.BlockSpec(memory_space=pltpu.SMEM)
    return pl.pallas_call(
        functools.partial(kernel, n),
        out_shape=jax.ShapeDtypeStruct((rows, width), BF16),
        in_specs=[smem, smem] + [vmem] * 10,
        out_specs=vmem,
        scratch_shapes=[
            pltpu.VMEM((n, slice_rows + EXTRA, DV), BF16),
            pltpu.VMEM((n, slice_rows + EXTRA, DV), BF16),
            pltpu.VMEM((n, slice_rows, DV), BF16),
            pltpu.VMEM((n, slice_rows, DV), BF16),
            pltpu.VMEM((n, rows, 2 * MC), BF16),
            pltpu.VMEM((rows, H * DK), BF16),
            pltpu.VMEM((rows, H * DV), BF16),
            pltpu.VMEM((rows, H * DK), BF16),
            pltpu.VMEM((rows, H * DV), F32),
            pltpu.VMEM((rows, width), BF16),
            pltpu.VMEM((rows, MC), BF16),
            pltpu.VMEM((PLANE * P_SIZE, 2 * MC), BF16),
            pltpu.VMEM((MH, rows, 128), F32),
            pltpu.VMEM((MH, rows, 128), F32),
            pltpu.VMEM((rows, MC), F32),
            pltpu.SemaphoreType.DMA((n,)),
            pltpu.SemaphoreType.DMA((n,)),
            pltpu.SemaphoreType.DMA((n,)),
            pltpu.SemaphoreType.DMA((n,)),
            pltpu.SemaphoreType.DMA((3, n)),
            pltpu.SemaphoreType.DMA((n,)),
        ],
        compiler_params=pltpu.CompilerParams(
            collective_id=0, has_side_effects=True, vmem_limit_bytes=56 * 2**20
        ),
    )(
        mem_index,
        mem_count,
        tokens,
        log_decay,
        w_rq,
        w_rk,
        w_rv,
        norm_gain.reshape(1, -1),
        w_mq,
        w_mk,
        w_mv,
        w_out,
    )


def solution(mesh):
    placed = (
        P(("groups", "tm"), None),
        P(None, ("groups", "tm")),
        P(("groups", "tm"), None),
        P(("groups", "tm")),
    ) + (P(),) * 8
    return jax.shard_map(
        functools.partial(on_device, mesh.shape["tm"]),
        mesh=mesh,
        in_specs=placed,
        out_specs=P(("groups", "tm"), None),
        check_vma=False,
    )
```

time: 294 us -> 82.5 us (0.28); the launches traced: 288 us -> 82.4 us
  waiting for transfers between devices: 85.4 us -> 0 us
  Pallas kernels: 0 us -> 80.5 us
  blocking collectives: 68.6 us -> 0 us
  local copies, waits for them, and re-layouts: 38.3 us -> 1.87 us
  matrix products: 34.8 us -> 0 us
  other arithmetic: 34.2 us -> 0 us
  between operations: 13.7 us -> 0.01 us
  starting transfers between devices: 12.6 us -> 0 us
    pallas_call x0 -> x1, Pallas kernels: none -> 80.5 us  [on_device(): pl.pallas_call(functools.partial(kernel, n), out_shape=jax.ShapeDtypeStru...]
    all_to_all x1 -> x0, blocking collectives: 51.5 us -> none  [on_device(): lax.all_to_all(outgoing_keys_table, 'tm', split_axis=0, concat_axis=0, ti...]
    all_gather x1 -> x0, waiting for transfers between devices: 45.5 us -> none  [entering(): everything = jax.tree.map(lambda part: lax.all_gather(part, axis), x)]
    all_to_all x2 -> x0, waiting for transfers between devices: 39.9 us -> none  [the longest x1 39.9 us: on_device(): lax.all_to_all(send_values, 'tm', split_axis=0, concat_axis=0, tiled=True)]
    dot_general x19 -> x0, matrix products: 31.3 us -> none  [the longest x1 7.29 us: on_device(): jnp.einsum('fhqk,fkhd->fqhd', probs, values_all, preferred_element_type=j...]
    select_n x21 -> x0, other arithmetic: 25.4 us -> none  [the longest x16 18.8 us: hop(): return jax.tree.map(lambda a, b: jnp.where(reached, a, b), new, before)]
    all_gather x1 -> x0, blocking collectives: 17 us -> none  [entering(): everything = jax.tree.map(lambda part: lax.all_gather(part, axis), x)]
    all_to_all x2 -> x0, starting transfers between devices: 12.6 us -> none  [the longest x1 6.39 us: on_device(): lax.all_to_all(wanted_here[:, None], 'tm', split_axis=0, concat_axis=0, t...]
  transfers between devices with their start and end apart: 3 -> 0, of which waited for: 2 -> 0; matrix products, arithmetic and copies ran while one was open for 3% -> 0% of each run, Pallas kernels for 0% -> 0%
where the time goes in v1:
time: 82.5 us; the launch traced here: 82.4 us
  Pallas kernels  80.5 us (98%)
  local copies, waits for them, and re-layouts  1.87 us (2%)
    pallas_call x1, Pallas kernels, on_device(): pl.pallas_call(functools.partial(kernel, n), out_shape=jax.ShapeDtypeStru...  80.5 us
    unnamed x1, local copies, waits for them, and re-layouts  1.87 us

profile of v1, /device:TPU:25, one launch (start us, length us, event | category | flops | bytes accessed | tf_op | source)
XLA Modules:
  0.0 82.4 jit_solution(4069612177245547930)
XLA Ops:
  0.0 80.5 %shard_map.118 = bf16[256,1024]{1,0:T(8,128)(2,1)} custom-call(s32[2,8]{1,0:T(2,128)} %idx_ref.1, s32[2]{0:T(128)} %cnt_ref.1, bf16[256,1024]{1,0:T(8,128)(2,1)} %tok_ref.1, f32[8,256]{1,0:T(8,128)} %ld_ref.1, bf16[1024,512]{1,0:T(8,128)(2,1)} %wrq_ref.1, bf16[1024,512]{1,0:T(8,128)(2,1)} %wrk_ref.1, bf16[1024,1024]{1,0:T(8,128)(2,1)} %wrv_ref.1, ...), custom_call_target="tpu_custom_call" | custom-call | tf_op jit(solution)/shard_map/pallas_call | solution.py:352
  80.5 1.9 %copy.14 = bf16[256,1024]{1,0:T(8,128)(2,1)} copy(bf16[256,1024]{1,0:T(8,128)(2,1)} %shard_map.118) | data formatting | bytes 1048576

commit v2 on v1

--- a/solution.py
+++ b/solution.py
@@ -36,14 +36,14 @@
     cnt_ref,
     tok_ref,
     ld_ref,
-    wrq_ref,
-    wrk_ref,
-    wrv_ref,
+    wrq_hbm,
+    wrk_hbm,
+    wrv_hbm,
     gain_ref,
-    wmq_ref,
-    wmk_ref,
-    wmv_ref,
-    wout_ref,
+    wmq_hbm,
+    wmk_hbm,
+    wmv_hbm,
+    wout_hbm,
     out_ref,
     msg_out,
     msg_in,
@@ -66,6 +66,14 @@
     recv2,
     send_kv,
     recv_kv,
+    wrq_ref,
+    wrk_ref,
+    wrv_ref,
+    wmq_ref,
+    wmk_ref,
+    wmv_ref,
+    wout_ref,
+    load_w,
 ):
     rows = tok_ref.shape[0]
     fpd = rows // P_SIZE
@@ -78,6 +86,19 @@
     p_y = (p + 2) % PLANE
     y_mate = z * PLANE + p_y
 
+    def load(i, src, dst):
+        return pltpu.make_async_copy(src, dst, load_w.at[i])
+
+    load_rk = load(0, wrk_hbm, wrk_ref)
+    load_rv = load(1, wrv_hbm, wrv_ref)
+    load_rq = load(2, wrq_hbm, wrq_ref)
+    load_mk = load(3, wmk_hbm, wmk_ref)
+    load_mv = load(4, wmv_hbm, wmv_ref)
+    load_mq = load(5, wmq_hbm, wmq_ref)
+    load_out = load(6, wout_hbm, wout_ref)
+    for copy in (load_rk, load_rv, load_rq, load_mk, load_mv, load_mq, load_out):
+        copy.start()
+
     barrier = pltpu.get_barrier_semaphore()
 
     def greet(i, carry):
@@ -87,7 +108,9 @@
     lax.fori_loop(1, n, greet, 0)
 
     tok = tok_ref[...]
+    load_rk.wait()
     k_s[...] = dot(tok, wrk_ref[...]).astype(BF16)
+    load_rv.wait()
     v_s[...] = dot(tok, wrv_ref[...]).astype(BF16)
 
     t_id = lax.broadcasted_iota(jnp.int32, (rows, rows), 0)
@@ -154,6 +177,7 @@
     lax.fori_loop(1, n, send_slices, 0)
     msg_in[me] = msg_out[me]
 
+    load_rq.wait()
     q_s[...] = (dot(tok, wrq_ref[...]).astype(BF16).astype(F32) * DK**-0.5).astype(BF16)
     for head in range(H):
         pair = head // 2
@@ -216,30 +240,39 @@
         hid_s[:, col] = (tok_ref[:, col].astype(F32) + y).astype(BF16)
 
     hid = hid_s[...]
+    load_mk.wait()
     kv[me, :, pl.ds(0, MC)] = dot(hid, wmk_ref[...]).astype(BF16)
+    load_mv.wait()
     kv[me, :, pl.ds(MC, MC)] = dot(hid, wmv_ref[...]).astype(BF16)
 
-    def copy_kv(slot, role, dst):
+    half_rows = rows // 2
+
+    def copy_kv(slot, half, role, dst):
+        part = kv.at[slot, pl.ds(half * half_rows, half_rows), :]
         return pltpu.make_async_remote_copy(
-            src_ref=kv.at[slot],
-            dst_ref=kv.at[slot],
-            send_sem=send_kv.at[role, slot],
-            recv_sem=recv_kv.at[slot],
+            src_ref=part,
+            dst_ref=part,
+            send_sem=send_kv.at[role, slot, half],
+            recv_sem=recv_kv.at[slot, half],
             device_id={"tm": dst},
         )
 
     up = (me + PLANE) % n
-
-    def pass_on(slot):
-        @pl.when(z < planes - 1)
-        def _():
-            copy_kv(slot, 0, up).start()
-
-        copy_kv(slot, 2, y_mate).start()
-        copy_kv(slot, 1, core_mate).start()
-
-    pass_on(me)
-
+    not_top = z < planes - 1
+    crossing = z * PLANE + p_y
+
+    def pass_on(slot, half):
+        @pl.when(not_top)
+        def _():
+            copy_kv(slot, half, 0, up).start()
+
+        copy_kv(slot, half, 1, core_mate).start()
+
+    for half in range(2):
+        copy_kv(me, half, 2, y_mate).start()
+        pass_on(me, half)
+
+    load_mq.wait()
     mq_s[...] = dot(hid, wmq_ref[...]).astype(BF16)
     key_scale = MD**-0.5
     own_frame = (t_id // P_SIZE) == (s_id // P_SIZE)
@@ -292,30 +325,66 @@
                 e.astype(BF16), sel_s[:, pl.ds(MC + h * MD, MD)]
             )
 
+    def wait_core(base):
+        near = base + (p + 1 - 2 * (p % 2))
+        diagonal = base + (p_y + 1 - 2 * (p_y % 2))
+        for half in range(2):
+            copy_kv(near, half, 1, core_mate).wait_recv()
+            copy_kv(diagonal, half, 1, core_mate).wait_recv()
+
     def plane_step(j, carry):
         base = (z - j) * PLANE
-        from_y = base + p_y
-        copy_kv(from_y, 2, y_mate).wait_recv()
-        copy_kv(from_y, 1, core_mate).start()
+
+        @pl.when(j != 1)
+        def _():
+            copy_kv(base + p_y, 0, 2, y_mate).wait_recv()
+            copy_kv(base + p_y, 0, 1, core_mate).start()
 
         @pl.when(j < z)
         def _():
             below = base - PLANE + p
-            copy_kv(below, 0, up).wait_recv()
-            pass_on(below)
-
-        near = base + (p + 1 - 2 * (p % 2))
-        copy_kv(near, 1, core_mate).wait_recv()
-        diagonal = base + (p_y + 1 - 2 * (p_y % 2))
-        copy_kv(diagonal, 1, core_mate).wait_recv()
+            copy_kv(below, 0, 0, up).wait_recv()
+            pass_on(below, 0)
+
+            @pl.when(j > 0)
+            def _():
+                copy_kv(below, 0, 2, y_mate).start()
+
+        copy_kv(base + p_y, 1, 2, y_mate).wait_recv()
+        copy_kv(base + p_y, 1, 1, core_mate).start()
+
+        @pl.when(j < z)
+        def _():
+            below = base - PLANE + p
+            copy_kv(below, 1, 0, up).wait_recv()
+            copy_kv(below, 1, 2, y_mate).start()
+            pass_on(below, 1)
+
+        @pl.when(jnp.logical_and(j == z, not_top))
+        def _():
+            copy_kv(crossing, 0, 0, up).start()
+
+        @pl.when(j != 1)
+        def _():
+            wait_core(base)
+            attend(base)
+
+        return carry
+
+    lax.fori_loop(0, z + 1, plane_step, 0)
+
+    @pl.when(z > 0)
+    def _():
+        base = (z - 1) * PLANE
+        copy_kv(base + p_y, 0, 0, up).wait_recv()
+        copy_kv(base + p_y, 0, 1, core_mate).start()
+        wait_core(base)
         attend(base)
-        return carry
-
-    lax.fori_loop(0, z + 1, plane_step, 0)
 
     for h in range(MH):
         col = pl.ds(h * MD, MD)
         mq_s[:, col] = (acc_s[:, col] / l_s[h][:, 0:1]).astype(BF16)
+    load_out.wait()
     projected = dot(mq_s[...], wout_ref[...])
     out_ref[...] = (hid_s[...].astype(F32) + projected).astype(BF16)
 
@@ -329,17 +398,27 @@
 
     def drain_kv(j, carry):
         base = (z - j) * PLANE
-
-        @pl.when(z < planes - 1)
-        def _():
-            copy_kv(base + p, 0, up).wait_send()
-
-        copy_kv(base + p, 2, y_mate).wait_send()
-        copy_kv(base + p, 1, core_mate).wait_send()
-        copy_kv(base + p_y, 1, core_mate).wait_send()
+        for half in range(2):
+
+            @pl.when(not_top)
+            def _():
+                copy_kv(base + p, half, 0, up).wait_send()
+
+            copy_kv(base + p, half, 1, core_mate).wait_send()
+            copy_kv(base + p_y, half, 1, core_mate).wait_send()
+
+        @pl.when(j != 1)
+        def _():
+            copy_kv(base + p, 0, 2, y_mate).wait_send()
+
+        copy_kv(base + p, 1, 2, y_mate).wait_send()
         return carry
 
     lax.fori_loop(0, z + 1, drain_kv, 0)
+
+    @pl.when(not_top)
+    def _():
+        copy_kv(crossing, 0, 0, up).wait_send()
 
 
 def on_device(
@@ -349,10 +428,12 @@
     slice_rows = 2 * H * DK // n
     vmem = pl.BlockSpec(memory_space=pltpu.VMEM)
     smem = pl.BlockSpec(memory_space=pltpu.SMEM)
+    hbm = pl.BlockSpec(memory_space=pl.ANY)
+    weights = (w_rq, w_rk, w_rv, w_mq, w_mk, w_mv, w_out)
     return pl.pallas_call(
         functools.partial(kernel, n),
         out_shape=jax.ShapeDtypeStruct((rows, width), BF16),
-        in_specs=[smem, smem] + [vmem] * 10,
+        in_specs=[smem, smem, vmem, vmem] + [hbm] * 3 + [vmem] + [hbm] * 4,
         out_specs=vmem,
         scratch_shapes=[
             pltpu.VMEM((n, slice_rows + EXTRA, DV), BF16),
@@ -374,9 +455,11 @@
             pltpu.SemaphoreType.DMA((n,)),
             pltpu.SemaphoreType.DMA((n,)),
             pltpu.SemaphoreType.DMA((n,)),
-            pltpu.SemaphoreType.DMA((3, n)),
-            pltpu.SemaphoreType.DMA((n,)),
-        ],
+            pltpu.SemaphoreType.DMA((3, n, 2)),
+            pltpu.SemaphoreType.DMA((n, 2)),
+        ]
+        + [pltpu.VMEM(w.shape, BF16) for w in weights]
+        + [pltpu.SemaphoreType.DMA((len(weights),))],
         compiler_params=pltpu.CompilerParams(
             collective_id=0, has_side_effects=True, vmem_limit_bytes=56 * 2**20
         ),

time: 82.5 us -> 78.9 us (0.956); the launches traced: 82.4 us -> 77.9 us
  Pallas kernels: 80.5 us -> 76 us
    pallas_call x1, Pallas kernels: 80.5 us -> 76 us  [on_device(): pl.pallas_call(functools.partial(kernel, n), out_shape=jax.ShapeDtypeStru...]
where the time goes in v2:
time: 78.9 us; the launch traced here: 77.9 us
  Pallas kernels  76 us (96%)
  local copies, waits for them, and re-layouts  1.87 us (2%)
    pallas_call x1, Pallas kernels, on_device(): pl.pallas_call(functools.partial(kernel, n), out_shape=jax.ShapeDtypeStru...  76 us
    unnamed x1, local copies, waits for them, and re-layouts  1.87 us

profile of v2, /device:TPU:25, one launch (start us, length us, event | category | flops | bytes accessed | tf_op | source)
XLA Modules:
  0.0 77.9 jit_solution(8954295240877279389)
XLA Ops:
  0.0 76.0 %shard_map.118 = bf16[256,1024]{1,0:T(8,128)(2,1)} custom-call(s32[2,8]{1,0:T(2,128)} %idx_ref.1, s32[2]{0:T(128)} %cnt_ref.1, bf16[256,1024]{1,0:T(8,128)(2,1)} %tok_ref.1, f32[8,256]{1,0:T(8,128)} %ld_ref.1, bf16[1024,512]{1,0:T(8,128)(2,1)} %wrq_hbm.1, bf16[1024,512]{1,0:T(8,128)(2,1)} %wrk_hbm.1, bf16[1024,1024]{1,0:T(8,128)(2,1)} %wrv_hbm.1, ...), custom_call_target="tpu_custom_call" | custom-call | tf_op jit(solution)/shard_map/pallas_call | solution.py:433
  76.0 1.9 %copy.14 = bf16[256,1024]{1,0:T(8,128)(2,1)} copy(bf16[256,1024]{1,0:T(8,128)(2,1)} %shard_map.118) | data formatting | bytes 1048576

commit v3 on v2

--- a/solution.py
+++ b/solution.py
@@ -239,12 +239,6 @@
         y = o * scale * gain_ref[:, col]
         hid_s[:, col] = (tok_ref[:, col].astype(F32) + y).astype(BF16)
 
-    hid = hid_s[...]
-    load_mk.wait()
-    kv[me, :, pl.ds(0, MC)] = dot(hid, wmk_ref[...]).astype(BF16)
-    load_mv.wait()
-    kv[me, :, pl.ds(MC, MC)] = dot(hid, wmv_ref[...]).astype(BF16)
-
     half_rows = rows // 2
 
     def copy_kv(slot, half, role, dst):
@@ -268,12 +262,17 @@
 
         copy_kv(slot, half, 1, core_mate).start()
 
+    load_mk.wait()
+    load_mv.wait()
     for half in range(2):
+        part = pl.ds(half * half_rows, half_rows)
+        kv[me, part, pl.ds(0, MC)] = dot(hid_s[part, :], wmk_ref[...]).astype(BF16)
+        kv[me, part, pl.ds(MC, MC)] = dot(hid_s[part, :], wmv_ref[...]).astype(BF16)
         copy_kv(me, half, 2, y_mate).start()
         pass_on(me, half)
 
     load_mq.wait()
-    mq_s[...] = dot(hid, wmq_ref[...]).astype(BF16)
+    mq_s[...] = dot(hid_s[...], wmq_ref[...]).astype(BF16)
     key_scale = MD**-0.5
     own_frame = (t_id // P_SIZE) == (s_id // P_SIZE)
     for h in range(MH):
@@ -286,34 +285,36 @@
         l_s[h] = jnp.broadcast_to(jnp.sum(e, axis=-1, keepdims=True), (rows, 128))
         acc_s[:, col] = dot(e.astype(BF16), kv[me, :, pl.ds(MC + h * MD, MD)])
 
-    keys = PLANE * P_SIZE
-    key_owner = lax.broadcasted_iota(jnp.int32, (P_SIZE, keys), 1) // P_SIZE
-
-    def attend(base):
+    def attend(owners):
+        keys = len(owners) * P_SIZE
+        slot = lax.broadcasted_iota(jnp.int32, (P_SIZE, keys), 1) // P_SIZE
+        key_owner = jnp.full((P_SIZE, keys), owners[0], jnp.int32)
+        for w in range(1, len(owners)):
+            key_owner = jnp.where(slot == w, owners[w], key_owner)
         live = []
-        wants = [jnp.int32(0)] * PLANE
+        wants = [jnp.int32(0)] * len(owners)
         for f in range(fpd):
             hit = jnp.full((P_SIZE, keys), NEG, F32)
             count = cnt_ref[f]
             for i in range(MEM):
                 frame = idx_ref[f, i]
-                owner = jnp.where(i < count, lax.div(frame, jnp.int32(fpd)), -1) - base
+                owner = jnp.where(i < count, lax.div(frame, jnp.int32(fpd)), -1)
                 local = lax.rem(frame, jnp.int32(fpd))
                 hit = jnp.where(key_owner == owner, 0.0, hit)
                 wants = [
-                    jnp.where(owner == w, local, wants[w]) for w in range(PLANE)
+                    jnp.where(owner == owners[w], local, wants[w]) for w in range(len(owners))
                 ]
             live.append(hit)
         bias = jnp.concatenate(live, axis=0)
-        for w in range(PLANE):
-            chosen = kv[base + w, pl.ds(0, P_SIZE), :]
+        for w in range(len(owners)):
+            chosen = kv[owners[w], pl.ds(0, P_SIZE), :]
             want = jnp.full((P_SIZE, 2 * MC), wants[w], jnp.int32)
             for f in range(1, fpd):
-                chosen = jnp.where(want == f, kv[base + w, pl.ds(f * P_SIZE, P_SIZE), :], chosen)
+                chosen = jnp.where(want == f, kv[owners[w], pl.ds(f * P_SIZE, P_SIZE), :], chosen)
             sel_s[pl.ds(w * P_SIZE, P_SIZE), :] = chosen
         for h in range(MH):
             col = pl.ds(h * MD, MD)
-            s = dot(mq_s[:, col], sel_s[:, pl.ds(h * MD, MD)], NT) * key_scale + bias
+            s = dot(mq_s[:, col], sel_s[pl.ds(0, keys), pl.ds(h * MD, MD)], NT) * key_scale + bias
             m_old = m_s[h][:, 0:1]
             m = jnp.maximum(m_old, jnp.max(s, axis=-1, keepdims=True))
             fade = jnp.exp(m_old - m)
@@ -322,15 +323,15 @@
             l_new = l_s[h][:, 0:1] * fade + jnp.sum(e, axis=-1, keepdims=True)
             l_s[h] = jnp.broadcast_to(l_new, (rows, 128))
             acc_s[:, col] = acc_s[:, col] * fade + dot(
-                e.astype(BF16), sel_s[:, pl.ds(MC + h * MD, MD)]
+                e.astype(BF16), sel_s[pl.ds(0, keys), pl.ds(MC + h * MD, MD)]
             )
 
-    def wait_core(base):
-        near = base + (p + 1 - 2 * (p % 2))
-        diagonal = base + (p_y + 1 - 2 * (p_y % 2))
+    p_near = p + 1 - 2 * (p % 2)
+    p_diagonal = p_y + 1 - 2 * (p_y % 2)
+
+    def wait_core(slot):
         for half in range(2):
-            copy_kv(near, half, 1, core_mate).wait_recv()
-            copy_kv(diagonal, half, 1, core_mate).wait_recv()
+            copy_kv(slot, half, 1, core_mate).wait_recv()
 
     def plane_step(j, carry):
         base = (z - j) * PLANE
@@ -364,10 +365,16 @@
         def _():
             copy_kv(crossing, 0, 0, up).start()
 
+        wait_core(base + p_near)
+
         @pl.when(j != 1)
         def _():
-            wait_core(base)
-            attend(base)
+            wait_core(base + p_diagonal)
+            attend([base + w for w in range(PLANE)])
+
+        @pl.when(j == 1)
+        def _():
+            attend([base + p, base + p_near])
 
         return carry
 
@@ -378,8 +385,8 @@
         base = (z - 1) * PLANE
         copy_kv(base + p_y, 0, 0, up).wait_recv()
         copy_kv(base + p_y, 0, 1, core_mate).start()
-        wait_core(base)
-        attend(base)
+        wait_core(base + p_diagonal)
+        attend([base + p_y, base + p_diagonal])
 
     for h in range(MH):
         col = pl.ds(h * MD, MD)

time: 78.9 us -> 79.4 us (level)
  no operation moved by 1% of the time
where the time goes in v3:
time: 79.4 us; the launch traced here: 78.4 us
  Pallas kernels  76.5 us (96%)
  local copies, waits for them, and re-layouts  1.87 us (2%)
    pallas_call x1, Pallas kernels, on_device(): pl.pallas_call(functools.partial(kernel, n), out_shape=jax.ShapeDtypeStru...  76.5 us
    unnamed x1, local copies, waits for them, and re-layouts  1.87 us

profile of v3, /device:TPU:25, one launch (start us, length us, event | category | flops | bytes accessed | tf_op | source)
XLA Modules:
  0.0 78.4 jit_solution(18412405332015420127)
XLA Ops:
  0.0 76.5 %shard_map.118 = bf16[256,1024]{1,0:T(8,128)(2,1)} custom-call(s32[2,8]{1,0:T(2,128)} %idx_ref.1, s32[2]{0:T(128)} %cnt_ref.1, bf16[256,1024]{1,0:T(8,128)(2,1)} %tok_ref.1, f32[8,256]{1,0:T(8,128)} %ld_ref.1, bf16[1024,512]{1,0:T(8,128)(2,1)} %wrq_hbm.1, bf16[1024,512]{1,0:T(8,128)(2,1)} %wrk_hbm.1, bf16[1024,1024]{1,0:T(8,128)(2,1)} %wrv_hbm.1, ...), custom_call_target="tpu_custom_call" | custom-call | tf_op jit(solution)/shard_map/pallas_call | solution.py:440
  76.5 1.9 %copy.14 = bf16[256,1024]{1,0:T(8,128)(2,1)} copy(bf16[256,1024]{1,0:T(8,128)(2,1)} %shard_map.118) | data formatting | bytes 1048576
